TPU v7x, 32 devices: a whole 2x2x4 slice. The times are simulated.
32 devices in a mesh: seq: 8 (over z, y), tensor: 2 (over x), group: 2 (over core).
Axes of the slice: x: 2, y: 2, z: 4, core: 2. Of those that a mesh axis runs over, the one named last changes fastest.
Arguments:
- prefill_queries: bfloat16 [512, 8192], P(None, 'tensor'), may hold values from -6 to 6
- cached_keys: bfloat16 [16384, 1024], P(('seq', 'group'), 'tensor'), may hold values from -6 to 6
- cached_values: bfloat16 [16384, 1024], P(('seq', 'group'), 'tensor'), may hold values from -6 to 6
- span_keys: bfloat16 [512, 1024], P(('seq', 'group'), 'tensor'), may hold values from -6 to 6
- span_values: bfloat16 [512, 1024], P(('seq', 'group'), 'tensor'), may hold values from -6 to 6
- out_weight: bfloat16 [8192, 8192], P('tensor', 'seq'), may hold values from -0.0625 to 0.0625
- decode_queries: bfloat16 [4, 32, 8192], P(None, 'group', 'tensor'), may hold values from -6 to 6
- decode_keys: bfloat16 [32, 2048, 1024], P('group', 'seq', 'tensor'), may hold values from -6 to 6
- decode_values: bfloat16 [32, 2048, 1024], P('group', 'seq', 'tensor'), may hold values from -6 to 6
- new_keys: bfloat16 [4, 32, 1024], P(None, 'group', 'tensor'), may hold values from -6 to 6
- new_values: bfloat16 [4, 32, 1024], P(None, 'group', 'tensor'), may hold values from -6 to 6
- request_lengths: int32 [32], replicated, may hold values from 1 to 2048
- row_requests: int32 [32], P('group'), may hold values from 0 to 31
- block_table: int32 [128, 1], replicated, may hold values from 0 to 15; in each aligned block of 128 rows (0 to 127, 128 to 255, ...) at most 16 rows name the same one
Outputs:
- prefill_out: bfloat16 [512, 8192], P('group', ('seq', 'tensor'))
- decode_out: bfloat16 [4, 32, 8192], P(None, 'group', ('seq', 'tensor'))
- landed_keys: bfloat16 [16, 16, 4, 1024], P(('seq', 'group'), None, None, 'tensor')
- landed_values: bfloat16 [16, 16, 4, 1024], P(('seq', 'group'), None, None, 'tensor')
Inputs may be any that keep to these rules, and one draw needn't show every extreme that they name: `block_table`: each owner receives at most 16 blocks, and some owner receives exactly 16; every owner receives at least one.
All inputs are finite; a program needn't handle non-finite values.
Results may differ from a plain program's by a relative error of at most 0.0052.
Values may be sent and summed in bfloat16 or wider, within the bound.
A program may use at most 128 MiB of HBM per device.

v0:
```python
import jax
import jax.numpy as jnp
from jax import lax
from jax.sharding import PartitionSpec as P

HEADS = 64
KV_HEADS = 8
HEAD = 128
SPAN = 512
BLOCK = 4


masked_score = -1e30


def prefill_scores(query_rows, keys_one, visible):
    scores = jnp.einsum(
        "qd,kd->qk", query_rows, keys_one, preferred_element_type=jnp.float32
    ) * HEAD ** (-0.5)
    return jnp.where(visible, scores, masked_score)


def body(
    prefill_queries,
    cached_keys,
    cached_values,
    span_keys,
    span_values,
    out_weight,
    decode_queries,
    decode_keys,
    decode_values,
    new_keys,
    new_values,
    request_lengths,
    row_requests,
    block_table,
):
    seq_count = lax.axis_size("seq")
    group_count = lax.axis_size("group")
    group_index = lax.axis_index("group")
    owner_index = lax.axis_index("seq") * group_count + group_index
    group_size = HEADS // KV_HEADS
    local_heads = prefill_queries.shape[1] // HEAD
    local_groups = cached_keys.shape[1] // HEAD
    span_rows = prefill_queries.shape[0]
    span_local = span_keys.shape[0]
    row_block = span_rows // (seq_count * group_count)
    half_rows = span_rows // group_count
    query_order = jnp.arange(span_rows, dtype=jnp.int32).reshape(group_count, seq_count, row_block)
    query_order = query_order.transpose(1, 0, 2).reshape(span_rows)
    queries = prefill_queries.reshape(group_count, seq_count, row_block, local_heads, HEAD)
    queries = queries.transpose(3, 1, 0, 2, 4).reshape(local_heads, span_rows, HEAD)
    key_rows = jnp.concatenate([cached_keys, span_keys], axis=0).reshape(-1, local_groups, HEAD)
    value_rows = jnp.concatenate([cached_values, span_values], axis=0).reshape(
        -1, local_groups, HEAD
    )
    key_position = jnp.concatenate(
        [
            jnp.full((cached_keys.shape[0],), -1, jnp.int32),
            owner_index * span_local + jnp.arange(span_local, dtype=jnp.int32),
        ]
    )
    visible = key_position[None, :] <= query_order[:, None]
    head_numbers = jnp.arange(local_heads, dtype=jnp.int32)

    def head_peak(inputs):
        query_rows, head_number = inputs
        keys_one = lax.dynamic_index_in_dim(key_rows, head_number // group_size, 1, keepdims=False)
        return jnp.max(prefill_scores(query_rows, keys_one, visible), axis=1)

    row_peak = lax.map(head_peak, (queries, head_numbers))
    row_peak = lax.pmax(row_peak, ("seq", "group"))

    def head_sums(inputs):
        query_rows, head_number, peak_one = inputs
        keys_one = lax.dynamic_index_in_dim(key_rows, head_number // group_size, 1, keepdims=False)
        values_one = lax.dynamic_index_in_dim(
            value_rows, head_number // group_size, 1, keepdims=False
        )
        scores = prefill_scores(query_rows, keys_one, visible)
        weights = jnp.where(visible, jnp.exp(scores - peak_one[:, None]), 0.0)
        weighted = jnp.dot(
            weights.astype(jnp.bfloat16), values_one, preferred_element_type=jnp.float32
        )
        return (weighted, jnp.sum(weights, axis=1))

    weighted, totals = lax.map(head_sums, (queries, head_numbers, row_peak))
    weighted, totals = lax.psum((weighted, totals), ("seq", "group"))
    weighted = lax.dynamic_index_in_dim(
        weighted.reshape(local_heads, seq_count, group_count, row_block, HEAD),
        group_index,
        2,
        keepdims=False,
    )
    totals = lax.dynamic_index_in_dim(
        totals.reshape(local_heads, seq_count, group_count, row_block),
        group_index,
        2,
        keepdims=False,
    )
    weighted = weighted.reshape(local_heads, half_rows, HEAD)
    totals = totals.reshape(local_heads, half_rows)
    attention = (weighted / totals[:, :, None]).astype(jnp.bfloat16)
    attention = attention.transpose(1, 0, 2).reshape(half_rows, local_heads * HEAD)
    span_partial = jnp.dot(attention, out_weight, preferred_element_type=jnp.float32)
    steps = decode_queries.shape[0]
    rows_local = decode_queries.shape[1]
    slots = decode_keys.shape[1]
    score_scale = HEAD ** (-0.5)
    step_queries = decode_queries.reshape(steps, rows_local, local_groups, group_size, HEAD)
    owned_keys = decode_keys.reshape(rows_local, slots, local_groups, HEAD)
    owned_values = decode_values.reshape(rows_local, slots, local_groups, HEAD)
    step_keys = new_keys.reshape(steps, rows_local, local_groups, HEAD)
    step_values = new_values.reshape(steps, rows_local, local_groups, HEAD)
    request_count = request_lengths.shape[0]
    picked = row_requests[:, None] == jnp.arange(request_count, dtype=jnp.int32)[None, :]
    row_length = jnp.sum(jnp.where(picked, request_lengths[None, :], 0), axis=1)
    position = lax.axis_index("seq") * slots + jnp.arange(slots, dtype=jnp.int32)
    live = (position[None, :] < row_length[:, None])[:, None, None, None, :]
    causal = (
        jnp.arange(steps, dtype=jnp.int32)[None, :] <= jnp.arange(steps, dtype=jnp.int32)[:, None]
    )
    cache_scores = (
        jnp.einsum(
            "trkgd,rskd->rkgts", step_queries, owned_keys, preferred_element_type=jnp.float32
        )
        * score_scale
    )
    cache_scores = jnp.where(live, cache_scores, masked_score)
    step_scores = (
        jnp.einsum("trkgd,urkd->rkgtu", step_queries, step_keys, preferred_element_type=jnp.float32)
        * score_scale
    )
    step_scores = jnp.where(causal, step_scores, masked_score)
    cache_peak = lax.pmax(jnp.max(cache_scores, axis=4), "seq")
    peak = jnp.maximum(cache_peak, jnp.max(step_scores, axis=4))
    cache_weights = jnp.where(live, jnp.exp(cache_scores - peak[..., None]), 0.0)
    step_weights = jnp.where(causal, jnp.exp(step_scores - peak[..., None]), 0.0)
    cache_sum = jnp.einsum(
        "rkgts,rskd->rkgtd",
        cache_weights.astype(jnp.bfloat16),
        owned_values,
        preferred_element_type=jnp.float32,
    )
    cache_sum, cache_total = lax.psum((cache_sum, jnp.sum(cache_weights, axis=4)), "seq")
    step_sum = jnp.einsum(
        "rkgtu,urkd->rkgtd",
        step_weights.astype(jnp.bfloat16),
        step_values,
        preferred_element_type=jnp.float32,
    )
    decode_total = cache_total + jnp.sum(step_weights, axis=4)
    decoded = ((cache_sum + step_sum) / decode_total[..., None]).astype(jnp.bfloat16)
    decoded = decoded.transpose(3, 0, 1, 2, 4).reshape(steps * rows_local, local_heads * HEAD)
    decode_partial = jnp.dot(decoded, out_weight, preferred_element_type=jnp.float32)
    span_part, decode_part = (
        lax.psum_scatter(span_partial, "tensor", scatter_dimension=1, tiled=True),
        lax.psum_scatter(decode_partial, "tensor", scatter_dimension=1, tiled=True),
    )
    prefill_out = span_part.astype(jnp.bfloat16)
    decode_out = decode_part.astype(jnp.bfloat16).reshape(steps, rows_local, -1)
    gathered_keys, gathered_values = (
        lax.all_gather(span_keys, ("seq", "group"), axis=0, tiled=True),
        lax.all_gather(span_values, ("seq", "group"), axis=0, tiled=True),
    )
    block_count = SPAN // BLOCK
    most_blocks = 2 * block_count // (seq_count * group_count)
    targets = block_table[:, 0]
    block_order = jnp.arange(block_count, dtype=jnp.int32)
    earlier = (targets[None, :] == targets[:, None]) & (block_order[None, :] < block_order[:, None])
    block_rank = jnp.sum(earlier.astype(jnp.int32), axis=1)
    slot_ids = jnp.arange(most_blocks, dtype=jnp.int32)
    chosen = (targets[None, :] == owner_index) & (block_rank[None, :] == slot_ids[:, None])
    chosen = chosen.astype(jnp.bfloat16)
    landed_keys = jnp.dot(
        chosen, gathered_keys.reshape(block_count, -1), preferred_element_type=jnp.float32
    )
    landed_values = jnp.dot(
        chosen, gathered_values.reshape(block_count, -1), preferred_element_type=jnp.float32
    )
    landed_keys = landed_keys.astype(jnp.bfloat16).reshape(1, most_blocks, BLOCK, -1)
    landed_values = landed_values.astype(jnp.bfloat16).reshape(1, most_blocks, BLOCK, -1)
    return (prefill_out, decode_out, landed_keys, landed_values)


def solution(mesh):
    placed = (
        P(None, "tensor"),
        P(("seq", "group"), "tensor"),
        P(("seq", "group"), "tensor"),
        P(("seq", "group"), "tensor"),
        P(("seq", "group"), "tensor"),
        P("tensor", "seq"),
        P(None, "group", "tensor"),
        P("group", "seq", "tensor"),
        P("group", "seq", "tensor"),
        P(None, "group", "tensor"),
        P(None, "group", "tensor"),
        P(),
        P("group"),
        P(),
    )
    return jax.shard_map(
        body,
        mesh=mesh,
        in_specs=placed,
        out_specs=(
            P("group", ("seq", "tensor")),
            P(None, "group", ("seq", "tensor")),
            P(("seq", "group"), None, None, "tensor"),
            P(("seq", "group"), None, None, "tensor"),
        ),
        check_vma=False,
    )
```

profile of v0, /device:TPU:26, one launch (start us, length us, event | category | flops | bytes accessed | tf_op | source)
XLA Modules:
  0.0 721.7 jit_solution(3154043799270645682)
XLA Ops:
  7.2 3.4 copy.84
  10.7 3.5 copy.58
  14.6 149.1 %while.28 = (s32[]{:T(128)}, f32[32,512]{1,0:T(8,128)S(1)}, bf16[32,512,128]{2,1,0:T(8,128)(2,1)}, s32[32]{0:T(128)S(1)}, bf16[1056,4,128]{2,0,1:T(8,128)(2,1)S(...) while((s32[]{:T(128)}, f32[32,512]{1,0:T(8,128)S(1)}, ...), condition=%wide.region_2.3_spmd.clone, body=%wide.region_0.2_spmd.clone.sunk | while | flops 140574224 | bytes 418633 | solution.py:72
  64.4 1.4 fusion.88
  69.0 1.4 fusion.88
  83.0 1.4 fusion.88
  87.7 1.4 fusion.88
  138.9 1.4 fusion.88
  143.6 1.4 fusion.88
  157.5 1.4 fusion.88
  162.2 1.4 fusion.88
  165.3 6.9 reshape.169
  172.6 3.9 bitcast_reduce_fusion
  176.5 35.8 %pmax.15 = f32[16,4,8,4]{2,3,1,0:T(4,128)S(1)} all-reduce(f32[16,4,8,4]{2,3,1,0:T(4,128)S(1)} %get-tuple-element.331), channel_id=1, replica_groups=mesh['seq'=8,'tensor'=2,'group'=2] {'seq'}, use_global_device_ids=true, to_apply=%region_12.13 | all-reduce | flops 2048 | bytes 16384 | tf_op jit(solution)/shard_map/pmax | solution.py:136
  212.4 7.0 reshape.172
  219.4 3.2 fusion.69
  222.7 4.1 fusion.25
  226.9 1.4 copy_bitcast_fusion
  228.3 23.3 %all-reduce.6.cloned.1.call-done = f32[32,512]{1,0:T(8,128)} async-done(((f32[32,512]{1,0:T(8,128)}), f32[32,512]{1,0:T(8,128)}) %all-reduce.6.cloned.1.call-update) | async-done | bytes 65552 | tf_op jit(solution)/shard_map/pmax | solution.py:73
  251.6 224.6 %while.29 = (s32[]{:T(128)}, f32[32,512,128]{2,1,0:T(8,128)}, f32[32,512]{1,0:T(8,128)S(1)}, bf16[32,512,128]{2,1,0:T(8,128)(2,1)}, s32[32]{0:T(128)S(1)}, /*ind...) while((s32[]{:T(128)}, f32[32,512,128]{2,1,0:T(8,128)}, ...), condition=%wide.region_6.7_spmd.clone, body=%wide.region_4.6_spmd.clone.sunk | while | flops 280608256 | bytes 3116521 | solution.py:88
  255.6 1.8 fusion.91
  262.6 1.8 fusion.91
  269.6 1.8 fusion.91
  276.6 1.8 fusion.91
  283.7 1.8 fusion.91
  290.7 1.8 fusion.91
  297.7 1.8 fusion.91
  304.8 1.8 fusion.91
  311.8 1.8 fusion.91
  318.8 1.8 fusion.91
  325.8 1.8 fusion.91
  332.9 1.8 fusion.91
  339.9 1.8 fusion.91
  346.9 1.8 fusion.91
  353.9 1.8 fusion.91
  360.9 1.8 fusion.91
  367.9 1.8 fusion.91
  374.9 1.8 fusion.91
  382.0 1.8 fusion.91
  389.0 1.8 fusion.91
  396.0 1.8 fusion.91
  403.0 1.8 fusion.91
  410.0 1.8 fusion.91
  417.0 1.8 fusion.91
  424.0 1.8 fusion.91
  431.0 1.8 fusion.91
  438.1 1.8 fusion.91
  445.1 1.8 fusion.91
  452.1 1.8 fusion.91
  459.1 1.8 fusion.91
  466.1 1.8 fusion.91
  473.1 1.8 fusion.91
  479.1 38.4 %psum.31 = f32[16,4,8,4]{2,3,1,0:T(4,128)S(1)} all-reduce(f32[16,4,8,4]{2,3,1,0:T(4,128)S(1)} %fusion.32), channel_id=1, replica_groups=mesh['seq'=8,'tensor'=2,'group'=2] {'seq'}, use_global_device_ids=true, to_apply=%region_16.17 | all-reduce | flops 2048 | bytes 16384 | tf_op jit(solution)/shard_map/psum | solution.py:146
  518.1 1.9 fusion.36
  520.4 5.7 fusion.71
  526.2 125.9 %all-reduce.10.cloned.1.call-done = (f32[32,8,2,32,128]{4,3,2,1,0:T(8,128)}, f32[32,8,2,32]{3,2,1,0:T(2,128)}) async-done(((f32[32,8,2,32,128]{4,3,2,1,0:T(8,128)}, f32[32,8,2,32]{3,2,1,0:T(2,128)}), (f32[32,8,2,32,128]{4,3,2,1,0:T(8,128)}, f32[32,8,2,32]{3,2,1,0:T(2,128)})) %all-reduce.10.cloned.1.call-update) | async-done | bytes 8454160 | tf_op jit(solution)/shard_map/psum | solution.py:89
  652.1 5.0 constant_dynamic-slice_fusion.1
  657.6 3.9 fusion.29
  661.5 3.3 copy.62
  664.7 6.8 fusion.70
  671.5 18.2 %all_gather.6 = bf16[512,512]{1,0:T(8,128)(2,1)S(1)} all-gather(bf16[32,512]{1,0:T(8,128)(2,1)S(1)} %copy-done.6), channel_id=1, replica_groups=mesh['seq'=8,'tensor'=2,'group'=2] {'seq','group'}, dimensions={0}, use_global_device_ids=true | all-gather | bytes 557056 | tf_op jit(solution)/shard_map/all_gather | solution.py:164
  691.1 19.5 %all_gather.7 = bf16[512,512]{1,0:T(8,128)(2,1)S(1)} all-gather(bf16[32,512]{1,0:T(8,128)(2,1)S(1)} %copy-done.7), channel_id=1, replica_groups=mesh['seq'=8,'tensor'=2,'group'=2] {'seq','group'}, dimensions={0}, use_global_device_ids=true | all-gather | bytes 557056 | tf_op jit(solution)/shard_map/all_gather | solution.py:165
  711.8 1.5 convert_element_type.39
  713.4 1.8 convert_element_type.35
  (291 shorter events, 145.4 us)
Async XLA Ops:
  7.2 244.5 %all-reduce.6.cloned.1.call-start = ((), (), s32[]{:S(2)}) async-start(), calls=%async_computation.2 | async-start | bytes 131072 | tf_op jit(solution)/shard_map/pmax | solution.py:73
  10.7 3.7 copy-start.1
  10.7 3.7 copy-start.6
  14.6 149.8 %copy-start.2 = (bf16[4,16,4096]{2,1,0:T(8,128)(2,1)S(1)}, bf16[4,16,4096]{2,1,0:T(8,128)(2,1)}, u32[]{:S(2)}) copy-start(bf16[4,16,4096]{2,1,0:T(8,128)(2,1)} %param.24) | copy-start | bytes 1572868
  163.6 0.6 copy-start.5
  163.7 8.6 %copy-start = (bf16[1056,4,128]{2,0,1:T(8,128)(2,1)}, bf16[1056,4,128]{2,0,1:T(8,128)(2,1)S(1)}, u32[]{:S(2)}) copy-start(bf16[1056,4,128]{2,0,1:T(8,128)(2,1)S(1)} %get-tuple-element.547) | copy-start | bytes 3244036
  164.3 353.8 %all-reduce.8.cloned.1.call-start = ((), (), s32[]{:S(2)}) async-start(), calls=%async_computation.4 | async-start | bytes 2097152 | tf_op jit(solution)/shard_map/psum | solution.py:146
  165.3 7.0 copy-start.11
  165.3 7.0 copy-start.12
  172.6 39.7 %copy-start.9 = (bf16[4,16,512]{2,1,0:T(8,128)(2,1)S(1)}, bf16[4,16,512]{2,1,0:T(8,128)(2,1)}, u32[]{:S(2)}) copy-start(bf16[4,16,512]{2,1,0:T(8,128)(2,1)} %param.27) | copy-start | bytes 196612
  212.3 7.0 copy-start.4
  222.7 4.2 copy-start.7
  226.8 425.3 %all-reduce.10.cloned.1.call-start = ((), (), s32[]{:S(2)}) async-start(), calls=%async_computation.6 | async-start | bytes 17301504 | tf_op jit(solution)/shard_map/psum | solution.py:89
  477.2 0.8 copy-start.10
  477.2 40.3 %copy-start.3 = (f32[16,4,8,4,4]{2,4,3,1,0:T(4,128)S(1)}, f32[16,4,8,4,4]{2,4,3,1,0:T(4,128)}, u32[]{:S(2)}) copy-start(f32[16,4,8,4,4]{2,4,3,1,0:T(4,128)} %get-tuple-element.334) | copy-start | bytes 98308
  477.2 234.6 %reduce-scatter.5.cloned.1.call-start = ((), (), s32[]{:S(2)}) async-start(), calls=%async_computation.5 | async-start | bytes 393216 | tf_op jit(solution)/shard_map/reduce_scatter | solution.py:159
  526.1 187.2 %reduce-scatter.3.cloned.1.call-start = ((), (), s32[]{:S(2)}) async-start(), calls=%async_computation.3 | async-start | bytes 1572864 | tf_op jit(solution)/shard_map/reduce_scatter | solution.py:158
  652.1 5.0 copy-start.8
  671.5 18.5 %copy-start.13 = (s32[128,1]{0,1:T(1,128)S(1)}, s32[128,1]{0,1:T(1,128)}, u32[]{:S(2)}) copy-start(s32[128,1]{0,1:T(1,128)} %param.31) | copy-start | bytes 1540
Sparse Core Ops, SparseCore 0:
  164.4 87.1 all-reduce.5
  255.1 76.8 all-reduce.7
  477.3 174.7 all-reduce.9
  654.2 11.6 reduce-scatter.4
  671.6 20.3 reduce-scatter.2
where the time goes:
time: 733 us; the launch traced here: 722 us
  loops' own time  169 us (23%)
  matrix products  167 us (23%)
  waiting for transfers between devices  149 us (20%)
  blocking collectives  112 us (15%)
  local copies, waits for them, and re-layouts  99.5 us (14%)
  between operations  14.1 us (2%)
  other arithmetic  10.9 us (1%)
    psum x1, waiting for transfers between devices, body(): weighted, totals = lax.psum((weighted, totals), ('seq', 'group'))  126 us
    dot_general x64, matrix products, prefill_scores(): jnp.einsum('qd,kd->qk', query_rows, keys_one, preferred_element_type=jnp....  102 us
    another operation x1, loops' own time, body(): weighted, totals = lax.map(head_sums, (queries, head_numbers, row_peak))  84.4 us
    another operation x1, loops' own time, body(): row_peak = lax.map(head_peak, (queries, head_numbers))  84.3 us
    dot_general x32, matrix products, head_sums(): jnp.dot(weights.astype(jnp.bfloat16), values_one, preferred_element_type=...  39.2 us
    psum x1, blocking collectives, body(): lax.psum((cache_sum, jnp.sum(cache_weights, axis=4)), 'seq')  38.4 us
    dynamic_slice x64, local copies, waits for them, and re-layouts, body(): row_peak = lax.map(head_peak, (queries, head_numbers))  37.7 us
    pmax x1, blocking collectives, body(): cache_peak = lax.pmax(jnp.max(cache_scores, axis=4), 'seq')  35.8 us
  transfers between devices with their start and end apart: 5, of which 2 were waited for; matrix products, arithmetic and copies ran while one was open for 28% of the time, Pallas kernels for 0%

commit v1 on v0

v1 whole, which is shorter than its diff:
```python
import functools
import math

import jax
import jax.numpy as jnp
from jax import lax
from jax.experimental import pallas as pl
from jax.experimental.pallas import tpu as pltpu
from jax.sharding import PartitionSpec as P

HEADS = 64
KV_HEADS = 8
HEAD = 128
BLOCK = 4
LANES = 128
SCALE = HEAD ** (-0.5)
SCALE2 = SCALE * math.log2(math.e)
masked_score = -1e30
MESH = pl.DeviceIdType.MESH
VMEM_LIMIT = 56 * 1024 * 1024


def dot_t(a, b):
    return lax.dot_general(a, b, (((1,), (1,)), ((), ())), preferred_element_type=jnp.float32)


def prefill_kernel(
    group_size, chunk, first_ref, q_ref, k_ref, v_ref, sk_ref, sv_ref, o_ref, lse_ref, va, sva
):
    step = pl.program_id(0)
    rows = q_ref.shape[0]
    span = sk_ref.shape[0]
    va[:, :HEAD] = v_ref[...]
    va[:, HEAD:] = jnp.ones((va.shape[0], HEAD), jnp.bfloat16)
    sva[:, :HEAD] = sv_ref[...]
    sva[:, HEAD:] = jnp.ones((span, HEAD), jnp.bfloat16)

    @pl.when(step == 0)
    def _():
        lse_ref[...] = jnp.zeros_like(lse_ref)

    first = first_ref[0]
    lane = lax.broadcasted_iota(jnp.int32, (chunk, LANES), 1)
    for head in range(group_size):
        columns = slice(head * HEAD, (head + 1) * HEAD)
        for start in range(0, rows, chunk):
            here = slice(start, start + chunk)
            q = q_ref[here, columns]
            s = dot_t(q, k_ref[...])
            t = dot_t(q, sk_ref[...])
            key = first + lax.broadcasted_iota(jnp.int32, (chunk, span), 1)
            query = start + lax.broadcasted_iota(jnp.int32, (chunk, span), 0)
            t = jnp.where(key <= query, t, masked_score)
            top = jnp.maximum(
                jnp.max(s, axis=1, keepdims=True), jnp.max(t, axis=1, keepdims=True)
            )
            shift = top * SCALE2
            p = jnp.exp2(s * SCALE2 - shift).astype(jnp.bfloat16)
            u = jnp.exp2(t * SCALE2 - shift).astype(jnp.bfloat16)
            acc = jnp.dot(p, va[...], preferred_element_type=jnp.float32)
            acc = acc + jnp.dot(u, sva[...], preferred_element_type=jnp.float32)
            total = acc[:, HEAD:]
            o_ref[here, columns] = (acc[:, :HEAD] / total).astype(jnp.bfloat16)
            lse = top * SCALE + jnp.log(total)
            lse_ref[here, :] = jnp.where(lane == step * group_size + head, lse, lse_ref[here, :])


def prefill_local(first, q, keys, values, span_keys, span_values):
    rows, width = q.shape
    local_groups = keys.shape[1] // HEAD
    group_size = HEADS // KV_HEADS
    chunk = min(256, rows)
    wide = group_size * HEAD
    by_group = lambda i: (0, i)
    return pl.pallas_call(
        functools.partial(prefill_kernel, group_size, chunk),
        grid=(local_groups,),
        out_shape=(
            jax.ShapeDtypeStruct((rows, width), jnp.bfloat16),
            jax.ShapeDtypeStruct((rows, LANES), jnp.float32),
        ),
        in_specs=[
            pl.BlockSpec(memory_space=pltpu.SMEM),
            pl.BlockSpec((rows, wide), by_group),
            pl.BlockSpec((keys.shape[0], HEAD), by_group),
            pl.BlockSpec((keys.shape[0], HEAD), by_group),
            pl.BlockSpec((span_keys.shape[0], HEAD), by_group),
            pl.BlockSpec((span_keys.shape[0], HEAD), by_group),
        ],
        out_specs=(
            pl.BlockSpec((rows, wide), by_group),
            pl.BlockSpec((rows, LANES), lambda i: (0, 0)),
        ),
        scratch_shapes=[
            pltpu.VMEM((keys.shape[0], 2 * HEAD), jnp.bfloat16),
            pltpu.VMEM((span_keys.shape[0], 2 * HEAD), jnp.bfloat16),
        ],
        compiler_params=pltpu.CompilerParams(vmem_limit_bytes=VMEM_LIMIT),
        cost_estimate=pl.CostEstimate(
            flops=4 * rows * width * keys.shape[0],
            bytes_accessed=4 * rows * width + 4 * keys.size,
            transcendentals=rows * width // HEAD * keys.shape[0],
        ),
    )(first, q, keys, values, span_keys, span_values)


def decode_kernel(
    group_size, length_ref, where_ref, q_ref, k_ref, v_ref, nk_ref, nv_ref, o_ref, lse_ref
):
    row = pl.program_id(0)
    slots = k_ref.shape[1]
    local_groups, many = q_ref.shape[1], q_ref.shape[2]
    steps = nk_ref.shape[2]
    length = length_ref[row] - where_ref[0] * slots
    live = lax.broadcasted_iota(jnp.int32, (many, slots), 1) < length
    query_step = lax.broadcasted_iota(jnp.int32, (many, steps), 0) // group_size
    token = lax.broadcasted_iota(jnp.int32, (many, steps), 1)
    seen = (token <= query_step) & (where_ref[0] == 0)
    for group in range(local_groups):
        columns = slice(group * HEAD, (group + 1) * HEAD)
        q = q_ref[0, group]
        s = jnp.where(live, dot_t(q, k_ref[0, :, columns]), masked_score)
        t = jnp.where(seen, dot_t(q, nk_ref[0, group]), masked_score)
        top = jnp.maximum(jnp.max(s, axis=1, keepdims=True), jnp.max(t, axis=1, keepdims=True))
        shift = top * SCALE2
        p = jnp.where(live, jnp.exp2(s * SCALE2 - shift), 0.0)
        u = jnp.where(seen, jnp.exp2(t * SCALE2 - shift), 0.0)
        total = jnp.sum(p, axis=1, keepdims=True) + jnp.sum(u, axis=1, keepdims=True)
        acc = jnp.dot(
            p.astype(jnp.bfloat16), v_ref[0, :, columns], preferred_element_type=jnp.float32
        )
        acc = acc + jnp.dot(
            u.astype(jnp.bfloat16), nv_ref[0, group], preferred_element_type=jnp.float32
        )
        any_key = total > 0.0
        safe = jnp.where(any_key, total, 1.0)
        o_ref[0, group] = (acc / safe).astype(jnp.bfloat16)
        lse = jnp.where(any_key, top * SCALE + jnp.log(safe), masked_score)
        lse_ref[0, group] = jnp.broadcast_to(lse, (many, LANES))


def decode_local(lengths, where, q, keys, values, new_keys, new_values):
    rows, local_groups, many, _ = q.shape
    slots, width = keys.shape[1:]
    steps = new_keys.shape[2]
    row4 = lambda i: (i, 0, 0, 0)
    row3 = lambda i: (i, 0, 0)
    return pl.pallas_call(
        functools.partial(decode_kernel, HEADS // KV_HEADS),
        grid=(rows,),
        out_shape=(
            jax.ShapeDtypeStruct(q.shape, jnp.bfloat16),
            jax.ShapeDtypeStruct((rows, local_groups, many, LANES), jnp.float32),
        ),
        in_specs=[
            pl.BlockSpec(memory_space=pltpu.SMEM),
            pl.BlockSpec(memory_space=pltpu.SMEM),
            pl.BlockSpec((1, local_groups, many, HEAD), row4),
            pl.BlockSpec((1, slots, width), row3),
            pl.BlockSpec((1, slots, width), row3),
            pl.BlockSpec((1, local_groups, steps, HEAD), row4),
            pl.BlockSpec((1, local_groups, steps, HEAD), row4),
        ],
        out_specs=(
            pl.BlockSpec((1, local_groups, many, HEAD), row4),
            pl.BlockSpec((1, local_groups, many, LANES), row4),
        ),
        compiler_params=pltpu.CompilerParams(vmem_limit_bytes=VMEM_LIMIT),
        cost_estimate=pl.CostEstimate(
            flops=4 * rows * many * slots * width,
            bytes_accessed=4 * keys.size,
            transcendentals=rows * local_groups * many * slots,
        ),
    )(lengths, where, q, keys, values, new_keys, new_values)


def merge_kernel(
    n, heads, o_ref, l_ref, od_ref, ld_ref, out_ref,
    xo, xl, cb, cl, rb, rl,
    xo_send, xo_recv, xl_send, xl_recv, ro_send, ro_recv, rl_send, rl_recv, g_send, g_recv,
):
    me = lax.axis_index("seq")
    mine = lax.axis_index("group")
    other = 1 - mine

    barrier = pltpu.get_barrier_semaphore()
    pl.semaphore_signal(barrier, inc=1, device_id={"group": other}, device_id_type=MESH)
    for k in range(1, n):
        pl.semaphore_signal(
            barrier, inc=1, device_id={"seq": lax.rem(me + k, n)}, device_id_type=MESH
        )
    pl.semaphore_wait(barrier, n)

    def chip_copies(k):
        s = lax.rem(me + 1 + k, n)
        return (
            pltpu.make_async_remote_copy(
                src_ref=o_ref.at[other, s], dst_ref=xo.at[s],
                send_sem=xo_send.at[k], recv_sem=xo_recv.at[k],
                device_id={"group": other}, device_id_type=MESH,
            ),
            pltpu.make_async_remote_copy(
                src_ref=l_ref.at[other, s], dst_ref=xl.at[s],
                send_sem=xl_send.at[k], recv_sem=xl_recv.at[k],
                device_id={"group": other}, device_id_type=MESH,
            ),
        )

    def seq_copies(k):
        s = lax.rem(me + 1 + k, n)
        return (
            pltpu.make_async_remote_copy(
                src_ref=cb.at[s], dst_ref=rb.at[k],
                send_sem=ro_send.at[k], recv_sem=ro_recv.at[k],
                device_id={"seq": s}, device_id_type=MESH,
            ),
            pltpu.make_async_remote_copy(
                src_ref=cl.at[s], dst_ref=rl.at[k],
                send_sem=rl_send.at[k], recv_sem=rl_recv.at[k],
                device_id={"seq": s}, device_id_type=MESH,
            ),
        )

    def gather_copy(k):
        return pltpu.make_async_remote_copy(
            src_ref=out_ref.at[me], dst_ref=out_ref.at[me],
            send_sem=g_send.at[k], recv_sem=g_recv.at[k],
            device_id={"seq": lax.rem(me + 1 + k, n)}, device_id_type=MESH,
        )

    def start_chip(k, carry):
        for copy in chip_copies(k):
            copy.start()
        return carry

    lax.fori_loop(0, n, start_chip, 0)

    def merge_pair(k):
        s = lax.rem(me + 1 + k, n)
        for copy in chip_copies(k):
            copy.wait_recv()
        la, lb = l_ref[mine, s], xl[s]
        top = jnp.maximum(la, lb)
        wa, wb = jnp.exp(la - top), jnp.exp(lb - top)
        total = wa + wb
        wa, wb = wa / total, wb / total
        cl[s] = jnp.concatenate([top + jnp.log(total), ld_ref[s]], axis=0)
        for head in range(heads):
            columns = slice(head * HEAD, (head + 1) * HEAD)
            both = (
                o_ref[mine, s, :, columns].astype(jnp.float32) * wa[:, head : head + 1]
                + xo[s, :, columns].astype(jnp.float32) * wb[:, head : head + 1]
            )
            both = jnp.concatenate([both, od_ref[s, :, columns].astype(jnp.float32)], axis=0)
            cb[s, :, columns] = both.astype(jnp.bfloat16)

    def pair_and_send(k, carry):
        merge_pair(k)
        for copy in seq_copies(k):
            copy.start()
        return carry

    lax.fori_loop(0, n - 1, pair_and_send, 0)
    merge_pair(n - 1)

    def wait_seq(k, carry):
        for copy in seq_copies(k):
            copy.wait_recv()
        return carry

    lax.fori_loop(0, n - 1, wait_seq, 0)
    logs = [cl[me]] + [rl[k] for k in range(n - 1)]
    top = functools.reduce(jnp.maximum, logs)
    weights = [jnp.exp(one - top) for one in logs]
    total = functools.reduce(jnp.add, weights)
    weights = [one / total for one in weights]
    for head in range(heads):
        columns = slice(head * HEAD, (head + 1) * HEAD)
        one_column = slice(head, head + 1)
        total = cb[me, :, columns].astype(jnp.float32) * weights[0][:, one_column]
        for k in range(n - 1):
            total = total + rb[k, :, columns].astype(jnp.float32) * weights[k + 1][:, one_column]
        out_ref[me, :, columns] = total.astype(jnp.bfloat16)

    def start_gather(k, carry):
        gather_copy(k).start()
        return carry

    lax.fori_loop(0, n - 1, start_gather, 0)

    def finish_chip(k, carry):
        for copy in chip_copies(k):
            copy.wait_send()
        return carry

    lax.fori_loop(0, n, finish_chip, 0)

    def finish(k, carry):
        for copy in seq_copies(k):
            copy.wait_send()
        gather_copy(k).wait()
        return carry

    lax.fori_loop(0, n - 1, finish, 0)


def merge(n, o, lse, od, lsed):
    _, _, span_block, width = o.shape
    rows = span_block + od.shape[1]
    vmem = pl.BlockSpec(memory_space=pltpu.VMEM)
    return pl.pallas_call(
        functools.partial(merge_kernel, n, width // HEAD),
        out_shape=jax.ShapeDtypeStruct((n, rows, width), jnp.bfloat16),
        in_specs=[vmem] * 4,
        out_specs=vmem,
        scratch_shapes=[
            pltpu.VMEM((n, span_block, width), jnp.bfloat16),
            pltpu.VMEM((n, span_block, LANES), jnp.float32),
            pltpu.VMEM((n, rows, width), jnp.bfloat16),
            pltpu.VMEM((n, rows, LANES), jnp.float32),
            pltpu.VMEM((n - 1, rows, width), jnp.bfloat16),
            pltpu.VMEM((n - 1, rows, LANES), jnp.float32),
        ]
        + [pltpu.SemaphoreType.DMA((n,))] * 10,
        compiler_params=pltpu.CompilerParams(
            collective_id=0, has_side_effects=True, vmem_limit_bytes=VMEM_LIMIT
        ),
    )(o, lse, od, lsed)


def body(
    prefill_queries,
    cached_keys,
    cached_values,
    span_keys,
    span_values,
    out_weight,
    decode_queries,
    decode_keys,
    decode_values,
    new_keys,
    new_values,
    request_lengths,
    row_requests,
    block_table,
):
    seq_count = lax.axis_size("seq")
    group_count = lax.axis_size("group")
    seq_index = lax.axis_index("seq")
    owner_index = seq_index * group_count + lax.axis_index("group")
    group_size = HEADS // KV_HEADS
    span_rows, width = prefill_queries.shape
    local_heads = width // HEAD
    local_groups = cached_keys.shape[1] // HEAD
    span_local = span_keys.shape[0]
    span_block = span_rows // (seq_count * group_count)

    both = jnp.concatenate([span_keys, span_values], axis=1)
    gathered = lax.all_gather(both, ("seq", "group"), axis=0, tiled=True)

    first = (owner_index * span_local).astype(jnp.int32).reshape(1)
    o, lse = prefill_local(
        first, prefill_queries, cached_keys, cached_values, span_keys, span_values
    )
    o = o.reshape(group_count, seq_count, span_block, width)
    lse = lse.reshape(group_count, seq_count, span_block, LANES)

    steps, rows_local = decode_queries.shape[:2]
    decode_rows = steps * rows_local
    step_queries = decode_queries.reshape(steps, rows_local, local_groups, group_size, HEAD)
    step_queries = step_queries.transpose(1, 2, 0, 3, 4).reshape(
        rows_local, local_groups, steps * group_size, HEAD
    )
    by_row = lambda x: x.reshape(steps, rows_local, local_groups, HEAD).transpose(1, 2, 0, 3)
    picked = (
        row_requests[:, None] == jnp.arange(request_lengths.shape[0], dtype=jnp.int32)[None, :]
    )
    row_length = jnp.sum(jnp.where(picked, request_lengths[None, :], 0), axis=1)
    od, lsed = decode_local(
        row_length.astype(jnp.int32),
        seq_index.astype(jnp.int32).reshape(1),
        step_queries,
        decode_keys,
        decode_values,
        by_row(new_keys),
        by_row(new_values),
    )
    decode_block = decode_rows // seq_count
    od = od.reshape(rows_local, local_groups, steps, group_size, HEAD)
    od = od.transpose(2, 0, 1, 3, 4).reshape(seq_count, decode_block, width)
    lsed = lsed[..., 0].reshape(rows_local, local_groups, steps, group_size)
    lsed = lsed.transpose(2, 0, 1, 3).reshape(decode_rows, local_heads)
    lsed = jnp.pad(lsed, ((0, 0), (0, LANES - local_heads)))
    lsed = lsed.reshape(seq_count, decode_block, LANES)

    attention = merge(seq_count, o, lse, od, lsed)
    attention = attention.reshape(seq_count * (span_block + decode_block), width)
    partial = jnp.dot(attention, out_weight, preferred_element_type=jnp.float32)
    part = lax.psum_scatter(partial, "tensor", scatter_dimension=1, tiled=True)
    part = part.astype(jnp.bfloat16).reshape(seq_count, span_block + decode_block, -1)
    prefill_out = part[:, :span_block].reshape(seq_count * span_block, -1)
    decode_out = part[:, span_block:].reshape(steps, rows_local, -1)

    block_count = span_rows // BLOCK
    most_blocks = 2 * block_count // (seq_count * group_count)
    targets = block_table[:, 0]
    block_order = jnp.arange(block_count, dtype=jnp.int32)
    earlier = (targets[None, :] == targets[:, None]) & (block_order[None, :] < block_order[:, None])
    block_rank = jnp.sum(earlier.astype(jnp.int32), axis=1)
    slot_ids = jnp.arange(most_blocks, dtype=jnp.int32)
    chosen = (targets[None, :] == owner_index) & (block_rank[None, :] == slot_ids[:, None])
    chosen = chosen.astype(jnp.bfloat16)
    landed = jnp.dot(
        chosen, gathered.reshape(block_count, -1), preferred_element_type=jnp.float32
    ).astype(jnp.bfloat16)
    landed = landed.reshape(1, most_blocks, BLOCK, 2, -1)
    return (prefill_out, decode_out, landed[:, :, :, 0], landed[:, :, :, 1])


def solution(mesh):
    placed = (
        P(None, "tensor"),
        P(("seq", "group"), "tensor"),
        P(("seq", "group"), "tensor"),
        P(("seq", "group"), "tensor"),
        P(("seq", "group"), "tensor"),
        P("tensor", "seq"),
        P(None, "group", "tensor"),
        P("group", "seq", "tensor"),
        P("group", "seq", "tensor"),
        P(None, "group", "tensor"),
        P(None, "group", "tensor"),
        P(),
        P("group"),
        P(),
    )
    return jax.shard_map(
        body,
        mesh=mesh,
        in_specs=placed,
        out_specs=(
            P("group", ("seq", "tensor")),
            P(None, "group", ("seq", "tensor")),
            P(("seq", "group"), None, None, "tensor"),
            P(("seq", "group"), None, None, "tensor"),
        ),
        check_vma=False,
    )
```

time: 733 us -> 258 us (0.35); the launches traced: 722 us -> 255 us
  Pallas kernels: 0 us -> 187 us
  loops' own time: 169 us -> 0 us
  matrix products: 167 us -> 8.35 us
  waiting for transfers between devices: 149 us -> 26.1 us
  blocking collectives: 112 us -> 0 us
  local copies, waits for them, and re-layouts: 99.5 us -> 13.7 us
    pallas_call x0 -> x3, Pallas kernels: none -> 187 us  [the longest x1 132 us: merge(): pl.pallas_call(functools.partial(merge_kernel, n, width // HEAD), out_sha...]
    another operation x2 -> x0, loops' own time: 169 us -> none  [the longest x1 84.4 us: body(): weighted, totals = lax.map(head_sums, (queries, head_numbers, row_peak))]
    dot_general x104 -> x2, matrix products: 167 us -> 8.35 us  [the longest x1 8.11 us: body(): partial = jnp.dot(attention, out_weight, preferred_element_type=jnp.float32)]
    psum x2 -> x0, waiting for transfers between devices: 126 us -> none  [the longest x1 126 us: body(): weighted, totals = lax.psum((weighted, totals), ('seq', 'group'))]
    dynamic_slice x98 -> x0, local copies, waits for them, and re-layouts: 66.4 us -> none  [the longest x64 37.7 us: body(): row_peak = lax.map(head_peak, (queries, head_numbers))]
    psum x1 -> x0, blocking collectives: 38.4 us -> none  [body(): lax.psum((cache_sum, jnp.sum(cache_weights, axis=4)), 'seq')]
    all_gather x2 -> x0, blocking collectives: 37.7 us -> none  [the longest x1 19.5 us: body(): lax.all_gather(span_values, ('seq', 'group'), axis=0, tiled=True)]
    pmax x1 -> x0, blocking collectives: 35.8 us -> none  [body(): cache_peak = lax.pmax(jnp.max(cache_scores, axis=4), 'seq')]
  transfers between devices with their start and end apart: 5 -> 2, of which waited for: 2 -> 1; matrix products, arithmetic and copies ran while one was open for 28% -> 9% of each run, Pallas kernels for 0% -> 73%
where the time goes in v1:
time: 258 us; the launch traced here: 255 us
  Pallas kernels  187 us (72%)
  waiting for transfers between devices  26.1 us (10%)
  between operations  15.6 us (6%)
  local copies, waits for them, and re-layouts  13.7 us (5%)
  matrix products  8.35 us (3%)
  other arithmetic  4.13 us (2%)
    pallas_call x1, Pallas kernels, merge(): pl.pallas_call(functools.partial(merge_kernel, n, width // HEAD), out_sha...  132 us
    pallas_call x1, Pallas kernels, prefill_local(): pl.pallas_call(functools.partial(prefill_kernel, group_size, chunk), grid...  34.1 us
    reduce_scatter x1, waiting for transfers between devices, body(): part = lax.psum_scatter(partial, 'tensor', scatter_dimension=1, tiled=True)  26.1 us
    pallas_call x1, Pallas kernels, decode_local(): pl.pallas_call(functools.partial(decode_kernel, HEADS // KV_HEADS), grid=...  20.5 us
    dot_general x1, matrix products, body(): partial = jnp.dot(attention, out_weight, preferred_element_type=jnp.float32)  8.11 us
  transfers between devices with their start and end apart: 2, of which 1 were waited for; matrix products, arithmetic and copies ran while one was open for 9% of the time, Pallas kernels for 73%

profile of v1, /device:TPU:26, one launch (start us, length us, event | category | flops | bytes accessed | tf_op | source)
XLA Modules:
  0.0 254.9 jit_solution(7644917424661277293)
XLA Ops:
  8.0 0.0 all-gather.2.cloned.1.call-start
  8.0 1.4 pad_maximum_fusion
  9.5 0.0 all-gather.2.cloned.1.call-update
  9.5 0.0 reduce-scatter.2.cloned.1.call-start
  9.5 0.9 reshape.79
  10.4 0.9 reshape.80
  11.3 1.1 copy.44
  12.4 0.9 copy.51
  13.4 0.8 copy_bitcast_fusion.4
  14.1 1.4 select_reduce_fusion.length_ref
  15.5 20.5 %shard_map.166 = (bf16[16,4,32,128]{3,2,1,0:T(8,128)(2,1)}, f32[16,4,32,128]{3,2,1,0:T(8,128)}) custom-call(s32[16]{0:T(128)} %select_reduce_fusion.length_ref, s32[1]{0:T(128)} %bitcast.3.where_ref, bf16[16,4,32,128]{3,2,1,0:T(8,128)(2,1)} %bitcast.47, bf16[16,256,512]{2,1,0:T(8,128)(2,1)} %k_ref.3, bf16[16,256,512]{2,1,0:T(8,128)(2,1)} %v_ref.3, ...), custom_call_target="tpu_custom_call" | custom-call | flops 268435456 | bytes 8388608 | tf_op jit(solution)/shard_map/pallas_call | solution.py:148
  36.0 1.1 copy_bitcast_fusion
  37.2 1.1 reshape.82.od_ref
  38.2 2.1 copy.36
  40.3 0.1 reshape.83
  40.4 0.1 copy.43
  40.5 0.6 pad_bitcast_fusion.ld_ref
  41.1 34.1 %shard_map.165 = (bf16[512,4096]{1,0:T(8,128)(2,1)}, f32[512,128]{1,0:T(8,128)}) custom-call(s32[1]{0:T(128)} %bitcast.first_ref, bf16[512,4096]{1,0:T(8,128)(2,1)} %q_ref.1, bf16[1024,512]{1,0:T(8,128)(2,1)} %k_ref.2, bf16[1024,512]{1,0:T(8,128)(2,1)} %v_ref.2, bf16[32,512]{1,0:T(8,128)(2,1)} %sk_ref.1, bf16[32,512]{1,0:T(8,128)(2,1)} %sv_ref.1), custom_call_target="tpu_custom_call" | custom-call | flops 8589934592 | bytes 10485760 | tf_op jit(solution)/shard_map/pallas_call | solution.py:75
  75.2 132.3 %shard_map.167 = bf16[8,40,4096]{2,1,0:T(8,128)(2,1)} custom-call(bf16[2,8,32,4096]{3,2,1,0:T(8,128)(2,1)} %bitcast.45, f32[2,8,32,128]{3,2,1,0:T(8,128)} %bitcast.55, bf16[8,8,4096]{2,1,0:T(8,128)(2,1)} %reshape.82.od_ref, f32[8,8,128]{2,1,0:T(8,128)} %pad_bitcast_fusion.ld_ref), custom_call_target="tpu_custom_call" | custom-call | tf_op jit(solution)/shard_map/pallas_call | solution.py:311
  207.5 0.0 copy-start
  207.6 8.1 %fusion.6 = f32[320,1024]{1,0:T(8,128)} fusion(bf16[320,4096]{1,0:T(8,128)(2,1)} %bitcast.46, bf16[4096,1024]{1,0:T(8,128)(2,1)} %param.19), kind=kOutput, calls=%fused_computation.20 | convolution fusion | flops 2684354560 | bytes 12320768 | tf_op jit(solution)/shard_map/dot_general | solution.py:398
  215.7 0.0 reduce-scatter.2.cloned.1.call-update
  215.7 0.0 copy-done
  215.7 0.2 convert_reduce_fusion
  215.9 0.0 all-gather.2.cloned.1.call-done
  215.9 1.7 reshape.89
  217.6 0.2 convolution_convert_fusion
  217.9 0.1 reshape.90
  218.0 0.2 fusion.5
  218.2 0.7 copy_bitcast_fusion.2
  218.9 26.1 %reduce-scatter.2.cloned.1.call-done = f32[320,512]{1,0:T(8,128)} async-done(((f32[320,1024]{1,0:T(8,128)}), f32[320,512]{1,0:T(8,128)}) %reduce-scatter.2.cloned.1.call-update) | async-done | bytes 655376 | tf_op jit(solution)/shard_map/reduce_scatter | solution.py:399
  245.0 1.1 convert_element_type.12
  246.1 0.7 slice.20
  246.8 0.6 slice.21
  (2 shorter events, 0.0 us)
Async XLA Ops:
  8.0 207.9 %all-gather.2.cloned.1.call-start = ((), (), s32[]{:S(2)}) async-start(), calls=%async_computation.2 | async-start | bytes 1114112 | tf_op jit(solution)/shard_map/all_gather | solution.py:359
  9.5 235.5 %reduce-scatter.2.cloned.1.call-start = ((), (), s32[]{:S(2)}) async-start(), calls=%async_computation.1 | async-start | bytes 1966080 | tf_op jit(solution)/shard_map/reduce_scatter | solution.py:399
  207.5 8.1 %copy-start = (s32[128,1]{0,1:T(1,128)S(1)}, s32[128,1]{0,1:T(1,128)}, u32[]{:S(2)}) copy-start(s32[128,1]{0,1:T(1,128)} %param.27) | copy-start | bytes 1540
Sparse Core Ops, SparseCore 0:
  11.8 37.9 all-gather.1
Sparse Core Ops, SparseCore 1:
  215.8 29.1 reduce-scatter.1

commit v2 on v1

--- a/solution.py
+++ b/solution.py
@@ -116,27 +116,27 @@
     query_step = lax.broadcasted_iota(jnp.int32, (many, steps), 0) // group_size
     token = lax.broadcasted_iota(jnp.int32, (many, steps), 1)
     seen = (token <= query_step) & (where_ref[0] == 0)
-    for group in range(local_groups):
-        columns = slice(group * HEAD, (group + 1) * HEAD)
-        q = q_ref[0, group]
-        s = jnp.where(live, dot_t(q, k_ref[0, :, columns]), masked_score)
-        t = jnp.where(seen, dot_t(q, nk_ref[0, group]), masked_score)
-        top = jnp.maximum(jnp.max(s, axis=1, keepdims=True), jnp.max(t, axis=1, keepdims=True))
-        shift = top * SCALE2
-        p = jnp.where(live, jnp.exp2(s * SCALE2 - shift), 0.0)
-        u = jnp.where(seen, jnp.exp2(t * SCALE2 - shift), 0.0)
-        total = jnp.sum(p, axis=1, keepdims=True) + jnp.sum(u, axis=1, keepdims=True)
-        acc = jnp.dot(
-            p.astype(jnp.bfloat16), v_ref[0, :, columns], preferred_element_type=jnp.float32
-        )
-        acc = acc + jnp.dot(
-            u.astype(jnp.bfloat16), nv_ref[0, group], preferred_element_type=jnp.float32
-        )
-        any_key = total > 0.0
-        safe = jnp.where(any_key, total, 1.0)
-        o_ref[0, group] = (acc / safe).astype(jnp.bfloat16)
-        lse = jnp.where(any_key, top * SCALE + jnp.log(safe), masked_score)
-        lse_ref[0, group] = jnp.broadcast_to(lse, (many, LANES))
+    columns = [slice(group * HEAD, (group + 1) * HEAD) for group in range(local_groups)]
+    groups = range(local_groups)
+    stack = lambda parts: jnp.concatenate(parts, axis=0)
+    s = stack([jnp.where(live, dot_t(q_ref[0, g], k_ref[0, :, columns[g]]), masked_score) for g in groups])
+    t = stack([jnp.where(seen, dot_t(q_ref[0, g], nk_ref[0, g]), masked_score) for g in groups])
+    top = jnp.maximum(jnp.max(s, axis=1, keepdims=True), jnp.max(t, axis=1, keepdims=True))
+    shift = top * SCALE2
+    p = jnp.where(s > 0.5 * masked_score, jnp.exp2(s * SCALE2 - shift), 0.0)
+    u = jnp.where(t > 0.5 * masked_score, jnp.exp2(t * SCALE2 - shift), 0.0)
+    total = jnp.sum(p, axis=1, keepdims=True) + jnp.sum(u, axis=1, keepdims=True)
+    any_key = total > 0.0
+    safe = jnp.where(any_key, total, 1.0)
+    lse = jnp.where(any_key, top * SCALE + jnp.log(safe), masked_score)
+    lse = jnp.broadcast_to(lse, (local_groups * many, LANES))
+    p, u, share = p.astype(jnp.bfloat16), u.astype(jnp.bfloat16), 1.0 / safe
+    for g in groups:
+        here = slice(g * many, (g + 1) * many)
+        acc = jnp.dot(p[here], v_ref[0, :, columns[g]], preferred_element_type=jnp.float32)
+        acc = acc + jnp.dot(u[here], nv_ref[0, g], preferred_element_type=jnp.float32)
+        o_ref[0, g] = (acc * share[here]).astype(jnp.bfloat16)
+        lse_ref[0, g] = lse[here]
 
 
 def decode_local(lengths, where, q, keys, values, new_keys, new_values):
@@ -176,75 +176,86 @@
 
 def merge_kernel(
     n, heads, o_ref, l_ref, od_ref, ld_ref, out_ref,
-    xo, xl, cb, cl, rb, rl,
-    xo_send, xo_recv, xl_send, xl_recv, ro_send, ro_recv, rl_send, rl_recv, g_send, g_recv,
+    xo, xl, cb, cl, co, yb, yl, zb, rb, rl,
+    xo_send, xo_recv, xl_send, xl_recv, yo_send, yo_recv, yl_send, yl_recv,
+    ro_send, ro_recv, rl_send, rl_recv, g_send, g_recv, f_send, f_recv,
 ):
     me = lax.axis_index("seq")
     mine = lax.axis_index("group")
     other = 1 - mine
+    nz = n // 2
+    z, y = me // 2, lax.rem(me, 2)
+    beside = z * 2 + 1 - y
+
+    def ahead(k):
+        return lax.rem(z + 1 + k, nz)
 
     barrier = pltpu.get_barrier_semaphore()
     pl.semaphore_signal(barrier, inc=1, device_id={"group": other}, device_id_type=MESH)
-    for k in range(1, n):
+    pl.semaphore_signal(barrier, inc=1, device_id={"seq": beside}, device_id_type=MESH)
+    for k in range(nz - 1):
         pl.semaphore_signal(
-            barrier, inc=1, device_id={"seq": lax.rem(me + k, n)}, device_id_type=MESH
-        )
-    pl.semaphore_wait(barrier, n)
-
-    def chip_copies(k):
-        s = lax.rem(me + 1 + k, n)
+            barrier, inc=1, device_id={"seq": ahead(k) * 2 + y}, device_id_type=MESH
+        )
+    pl.semaphore_wait(barrier, nz + 1)
+
+    def send(src, dst, sends, recvs, k, device):
+        return pltpu.make_async_remote_copy(
+            src_ref=src, dst_ref=dst, send_sem=sends.at[k], recv_sem=recvs.at[k],
+            device_id=device, device_id_type=MESH,
+        )
+
+    def chip_copies(k, s):
+        there = {"group": other}
         return (
-            pltpu.make_async_remote_copy(
-                src_ref=o_ref.at[other, s], dst_ref=xo.at[s],
-                send_sem=xo_send.at[k], recv_sem=xo_recv.at[k],
-                device_id={"group": other}, device_id_type=MESH,
-            ),
-            pltpu.make_async_remote_copy(
-                src_ref=l_ref.at[other, s], dst_ref=xl.at[s],
-                send_sem=xl_send.at[k], recv_sem=xl_recv.at[k],
-                device_id={"group": other}, device_id_type=MESH,
-            ),
-        )
-
-    def seq_copies(k):
-        s = lax.rem(me + 1 + k, n)
+            send(o_ref.at[other, s], xo.at[s], xo_send, xo_recv, k, there),
+            send(l_ref.at[other, s], xl.at[s], xl_send, xl_recv, k, there),
+        )
+
+    def y_copies(k):
+        there = {"seq": beside}
         return (
-            pltpu.make_async_remote_copy(
-                src_ref=cb.at[s], dst_ref=rb.at[k],
-                send_sem=ro_send.at[k], recv_sem=ro_recv.at[k],
-                device_id={"seq": s}, device_id_type=MESH,
-            ),
-            pltpu.make_async_remote_copy(
-                src_ref=cl.at[s], dst_ref=rl.at[k],
-                send_sem=rl_send.at[k], recv_sem=rl_recv.at[k],
-                device_id={"seq": s}, device_id_type=MESH,
-            ),
-        )
-
-    def gather_copy(k):
-        return pltpu.make_async_remote_copy(
-            src_ref=out_ref.at[me], dst_ref=out_ref.at[me],
-            send_sem=g_send.at[k], recv_sem=g_recv.at[k],
-            device_id={"seq": lax.rem(me + 1 + k, n)}, device_id_type=MESH,
-        )
+            send(cb.at[k], yb.at[k], yo_send, yo_recv, k, there),
+            send(cl.at[k], yl.at[k], yl_send, yl_recv, k, there),
+        )
+
+    def z_copies(k):
+        there = {"seq": ahead(k) * 2 + y}
+        return (
+            send(zb.at[k], rb.at[k], ro_send, ro_recv, k, there),
+            send(cl.at[nz + k], rl.at[k], rl_send, rl_recv, k, there),
+        )
+
+    def far(k):
+        return ahead(k) * 2 + 1 - y
+
+    def near(k):
+        return ahead(k) * 2 + y
 
     def start_chip(k, carry):
-        for copy in chip_copies(k):
+        for copy in chip_copies(k, far(k)):
             copy.start()
         return carry
 
-    lax.fori_loop(0, n, start_chip, 0)
-
-    def merge_pair(k):
-        s = lax.rem(me + 1 + k, n)
-        for copy in chip_copies(k):
-            copy.wait_recv()
-        la, lb = l_ref[mine, s], xl[s]
+    def start_chip_near(k, carry):
+        for copy in chip_copies(nz + k, near(k)):
+            copy.start()
+        return carry
+
+    lax.fori_loop(0, nz, start_chip, 0)
+    lax.fori_loop(0, nz, start_chip_near, 0)
+
+    def pair_weights(la, lb):
         top = jnp.maximum(la, lb)
         wa, wb = jnp.exp(la - top), jnp.exp(lb - top)
         total = wa + wb
-        wa, wb = wa / total, wb / total
-        cl[s] = jnp.concatenate([top + jnp.log(total), ld_ref[s]], axis=0)
+        return wa / total, wb / total, top + jnp.log(total)
+
+    def merge_chip(k, slot, s, store):
+        for copy in chip_copies(slot, s):
+            copy.wait_recv()
+        wa, wb, log = pair_weights(l_ref[mine, s], xl[s])
+        cl[slot] = jnp.concatenate([log, ld_ref[s]], axis=0)
         for head in range(heads):
             columns = slice(head * HEAD, (head + 1) * HEAD)
             both = (
@@ -252,24 +263,51 @@
                 + xo[s, :, columns].astype(jnp.float32) * wb[:, head : head + 1]
             )
             both = jnp.concatenate([both, od_ref[s, :, columns].astype(jnp.float32)], axis=0)
-            cb[s, :, columns] = both.astype(jnp.bfloat16)
-
-    def pair_and_send(k, carry):
-        merge_pair(k)
-        for copy in seq_copies(k):
+            store[k, :, columns] = both.astype(store.dtype)
+
+    def phase_far(k, carry):
+        merge_chip(k, k, far(k), cb)
+        for copy in y_copies(k):
             copy.start()
         return carry
 
-    lax.fori_loop(0, n - 1, pair_and_send, 0)
-    merge_pair(n - 1)
-
-    def wait_seq(k, carry):
-        for copy in seq_copies(k):
+    def phase_near(k, carry):
+        merge_chip(k, nz + k, near(k), co)
+        return carry
+
+    lax.fori_loop(0, nz, phase_far, 0)
+    lax.fori_loop(0, nz, phase_near, 0)
+
+    def merge_y(k):
+        for copy in y_copies(k):
             copy.wait_recv()
-        return carry
-
-    lax.fori_loop(0, n - 1, wait_seq, 0)
-    logs = [cl[me]] + [rl[k] for k in range(n - 1)]
+        wa, wb, log = pair_weights(cl[nz + k], yl[k])
+        cl[nz + k] = log
+        for head in range(heads):
+            columns = slice(head * HEAD, (head + 1) * HEAD)
+            both = (
+                co[k, :, columns] * wa[:, head : head + 1]
+                + yb[k, :, columns].astype(jnp.float32) * wb[:, head : head + 1]
+            )
+            co[k, :, columns] = both
+            zb[k, :, columns] = both.astype(jnp.bfloat16)
+
+    def phase_y(k, carry):
+        merge_y(k)
+        for copy in z_copies(k):
+            copy.start()
+        return carry
+
+    lax.fori_loop(0, nz - 1, phase_y, 0)
+    merge_y(nz - 1)
+
+    def wait_z(k, carry):
+        for copy in z_copies(k):
+            copy.wait_recv()
+        return carry
+
+    lax.fori_loop(0, nz - 1, wait_z, 0)
+    logs = [cl[n - 1]] + [rl[k] for k in range(nz - 1)]
     top = functools.reduce(jnp.maximum, logs)
     weights = [jnp.exp(one - top) for one in logs]
     total = functools.reduce(jnp.add, weights)
@@ -277,31 +315,99 @@
     for head in range(heads):
         columns = slice(head * HEAD, (head + 1) * HEAD)
         one_column = slice(head, head + 1)
-        total = cb[me, :, columns].astype(jnp.float32) * weights[0][:, one_column]
-        for k in range(n - 1):
+        total = co[nz - 1, :, columns] * weights[0][:, one_column]
+        for k in range(nz - 1):
             total = total + rb[k, :, columns].astype(jnp.float32) * weights[k + 1][:, one_column]
         out_ref[me, :, columns] = total.astype(jnp.bfloat16)
 
+    def gather_z(k):
+        return send(
+            out_ref.at[me], out_ref.at[me], g_send, g_recv, k, {"seq": ahead(k) * 2 + y}
+        )
+
+    def forward(k):
+        s = lax.rem(z - 1 - k + nz, nz) * 2 + y
+        return send(out_ref.at[s], out_ref.at[s], f_send, f_recv, k, {"seq": beside})
+
+    forward_own = send(out_ref.at[me], out_ref.at[me], f_send, f_recv, nz - 1, {"seq": beside})
+
     def start_gather(k, carry):
-        gather_copy(k).start()
-        return carry
-
-    lax.fori_loop(0, n - 1, start_gather, 0)
-
-    def finish_chip(k, carry):
-        for copy in chip_copies(k):
+        gather_z(k).start()
+        return carry
+
+    forward_own.start()
+    lax.fori_loop(0, nz - 1, start_gather, 0)
+
+    def pass_on(k, carry):
+        gather_z(k).wait_recv()
+        forward(k).start()
+        return carry
+
+    lax.fori_loop(0, nz - 1, pass_on, 0)
+
+    def finish(k, carry):
+        for copy in chip_copies(k, far(k)) + chip_copies(nz + k, near(k)) + y_copies(k):
             copy.wait_send()
         return carry
 
-    lax.fori_loop(0, n, finish_chip, 0)
-
-    def finish(k, carry):
-        for copy in seq_copies(k):
+    def finish_z(k, carry):
+        for copy in z_copies(k):
             copy.wait_send()
-        gather_copy(k).wait()
-        return carry
-
-    lax.fori_loop(0, n - 1, finish, 0)
+        gather_z(k).wait_send()
+        forward(k).wait()
+        return carry
+
+    lax.fori_loop(0, nz, finish, 0)
+    lax.fori_loop(0, nz - 1, finish_z, 0)
+    forward_own.wait()
+
+
+def add_kernel(n, p_ref, out_ref, sb, rb, send_sem, recv_sem):
+    me = lax.axis_index("tensor")
+    barrier = pltpu.get_barrier_semaphore()
+    for k in range(1, n):
+        pl.semaphore_signal(
+            barrier, inc=1, device_id={"tensor": lax.rem(me + k, n)}, device_id_type=MESH
+        )
+    pl.semaphore_wait(barrier, n - 1)
+
+    def copy(k):
+        return pltpu.make_async_remote_copy(
+            src_ref=sb.at[k], dst_ref=rb.at[k], send_sem=send_sem.at[k], recv_sem=recv_sem.at[k],
+            device_id={"tensor": lax.rem(me + 1 + k, n)}, device_id_type=MESH,
+        )
+
+    for k in range(n - 1):
+        sb[k] = p_ref[lax.rem(me + 1 + k, n)].astype(jnp.bfloat16)
+        copy(k).start()
+    for k in range(n - 1):
+        copy(k).wait_recv()
+    total = p_ref[me]
+    for k in range(n - 1):
+        total = total + rb[k].astype(jnp.float32)
+    out_ref[...] = total.astype(jnp.bfloat16)
+    for k in range(n - 1):
+        copy(k).wait_send()
+
+
+def add_tensor(n, partial):
+    _, rows, columns = partial.shape
+    vmem = pl.BlockSpec(memory_space=pltpu.VMEM)
+    return pl.pallas_call(
+        functools.partial(add_kernel, n),
+        out_shape=jax.ShapeDtypeStruct((rows, columns), jnp.bfloat16),
+        in_specs=[vmem],
+        out_specs=vmem,
+        scratch_shapes=[
+            pltpu.VMEM((n - 1, rows, columns), jnp.bfloat16),
+            pltpu.VMEM((n - 1, rows, columns), jnp.bfloat16),
+            pltpu.SemaphoreType.DMA((n - 1,)),
+            pltpu.SemaphoreType.DMA((n - 1,)),
+        ],
+        compiler_params=pltpu.CompilerParams(
+            collective_id=1, has_side_effects=True, vmem_limit_bytes=VMEM_LIMIT
+        ),
+    )(partial)
 
 
 def merge(n, o, lse, od, lsed):
@@ -316,12 +422,16 @@
         scratch_shapes=[
             pltpu.VMEM((n, span_block, width), jnp.bfloat16),
             pltpu.VMEM((n, span_block, LANES), jnp.float32),
-            pltpu.VMEM((n, rows, width), jnp.bfloat16),
+            pltpu.VMEM((n // 2, rows, width), jnp.bfloat16),
             pltpu.VMEM((n, rows, LANES), jnp.float32),
-            pltpu.VMEM((n - 1, rows, width), jnp.bfloat16),
-            pltpu.VMEM((n - 1, rows, LANES), jnp.float32),
+            pltpu.VMEM((n // 2, rows, width), jnp.float32),
+            pltpu.VMEM((n // 2, rows, width), jnp.bfloat16),
+            pltpu.VMEM((n // 2, rows, LANES), jnp.float32),
+            pltpu.VMEM((n // 2, rows, width), jnp.bfloat16),
+            pltpu.VMEM((n // 2, rows, width), jnp.bfloat16),
+            pltpu.VMEM((n // 2, rows, LANES), jnp.float32),
         ]
-        + [pltpu.SemaphoreType.DMA((n,))] * 10,
+        + [pltpu.SemaphoreType.DMA((n,))] * 16,
         compiler_params=pltpu.CompilerParams(
             collective_id=0, has_side_effects=True, vmem_limit_bytes=VMEM_LIMIT
         ),
@@ -396,8 +506,9 @@
     attention = merge(seq_count, o, lse, od, lsed)
     attention = attention.reshape(seq_count * (span_block + decode_block), width)
     partial = jnp.dot(attention, out_weight, preferred_element_type=jnp.float32)
-    part = lax.psum_scatter(partial, "tensor", scatter_dimension=1, tiled=True)
-    part = part.astype(jnp.bfloat16).reshape(seq_count, span_block + decode_block, -1)
+    tensor_count = lax.axis_size("tensor")
+    partial = partial.reshape(partial.shape[0], tensor_count, -1).transpose(1, 0, 2)
+    part = add_tensor(tensor_count, partial).reshape(seq_count, span_block + decode_block, -1)
     prefill_out = part[:, :span_block].reshape(seq_count * span_block, -1)
     decode_out = part[:, span_block:].reshape(steps, rows_local, -1)
 

time: 258 us -> 210 us (0.81)
  Pallas kernels: 187 us -> 156 us
  waiting for transfers between devices: 26.1 us -> 0.04 us
  local copies, waits for them, and re-layouts: 13.7 us -> 26.7 us
    pallas_call x1, Pallas kernels: 132 us -> 97.4 us  [merge(): pl.pallas_call(functools.partial(merge_kernel, n, width // HEAD), out_sha...]
    reduce_scatter x1 -> x0, waiting for transfers between devices: 26.1 us -> none  [body(): part = lax.psum_scatter(partial, 'tensor', scatter_dimension=1, tiled=True)]
    dot_general x0 -> x1, local copies, waits for them, and re-layouts: none -> 11.2 us  [body(): partial = jnp.dot(attention, out_weight, preferred_element_type=jnp.float32)]
    pallas_call x0 -> x1, Pallas kernels: none -> 10.8 us  [add_tensor(): pl.pallas_call(functools.partial(add_kernel, n), out_shape=jax.ShapeDtype...]
    pallas_call x1, Pallas kernels: 20.5 us -> 14 us  [decode_local(): pl.pallas_call(functools.partial(decode_kernel, HEADS // KV_HEADS), grid=...]
  transfers between devices with their start and end apart: 2 -> 1, of which waited for: 1 -> 0; matrix products, arithmetic and copies ran while one was open for 9% -> 16% of each run, Pallas kernels for 73% -> 75%
where the time goes in v2:
time: 210 us; the launch traced here: 209 us
  Pallas kernels  156 us (74%)
  local copies, waits for them, and re-layouts  26.7 us (13%)
  between operations  14.1 us (7%)
  matrix products  8.47 us (4%)
  other arithmetic  2.94 us (1%)
    pallas_call x1, Pallas kernels, merge(): pl.pallas_call(functools.partial(merge_kernel, n, width // HEAD), out_sha...  97.4 us
    pallas_call x1, Pallas kernels, prefill_local(): pl.pallas_call(functools.partial(prefill_kernel, group_size, chunk), grid...  34.1 us
    pallas_call x1, Pallas kernels, decode_local(): pl.pallas_call(functools.partial(decode_kernel, HEADS // KV_HEADS), grid=...  14 us
    dot_general x1, local copies, waits for them, and re-layouts, body(): partial = jnp.dot(attention, out_weight, preferred_element_type=jnp.float32)  11.2 us
    pallas_call x1, Pallas kernels, add_tensor(): pl.pallas_call(functools.partial(add_kernel, n), out_shape=jax.ShapeDtype...  10.8 us
    dot_general x1, matrix products, body(): partial = jnp.dot(attention, out_weight, preferred_element_type=jnp.float32)  8.23 us
  transfers between devices with their start and end apart: 1, of which 0 were waited for; matrix products, arithmetic and copies ran while one was open for 16% of the time, Pallas kernels for 75%

profile of v2, /device:TPU:26, one launch (start us, length us, event | category | flops | bytes accessed | tf_op | source)
XLA Modules:
  0.0 208.6 jit_solution(2770303088634221790)
XLA Ops:
  7.2 0.0 all-gather.2.cloned.1.call-start
  7.2 1.4 pad_maximum_fusion
  8.6 0.0 all-gather.2.cloned.1.call-update
  8.6 0.9 reshape.81
  9.5 0.9 reshape.82
  10.4 1.1 copy.48
  11.5 0.9 copy.55
  12.5 0.8 copy_bitcast_fusion.4
  13.2 1.4 select_reduce_fusion.length_ref
  14.6 14.0 %shard_map.166 = (bf16[16,4,32,128]{3,2,1,0:T(8,128)(2,1)}, f32[16,4,32,128]{3,2,1,0:T(8,128)}) custom-call(s32[16]{0:T(128)} %select_reduce_fusion.length_ref, s32[1]{0:T(128)} %bitcast.3.where_ref, bf16[16,4,32,128]{3,2,1,0:T(8,128)(2,1)} %bitcast.55, bf16[16,256,512]{2,1,0:T(8,128)(2,1)} %k_ref.3, bf16[16,256,512]{2,1,0:T(8,128)(2,1)} %v_ref.3, ...), custom_call_target="tpu_custom_call" | custom-call | flops 268435456 | bytes 8388608 | tf_op jit(solution)/shard_map/pallas_call | solution.py:148
  28.6 1.1 copy_bitcast_fusion
  29.7 1.0 reshape.84.od_ref
  30.8 2.1 copy.38
  32.9 0.1 reshape.85
  33.0 0.1 copy.47
  33.0 0.6 pad_bitcast_fusion.ld_ref
  33.7 11.2 %copy.44 = bf16[1024,4096]{1,0:T(8,128)(2,1)} copy(bf16[1024,4096]{0,1:T(8,128)(2,1)} %bitcast.51) | data formatting | bytes 16777216 | tf_op jit(solution)/shard_map/dot_general | solution.py:508
  44.9 34.1 %shard_map.165 = (bf16[512,4096]{1,0:T(8,128)(2,1)}, f32[512,128]{1,0:T(8,128)}) custom-call(s32[1]{0:T(128)} %bitcast.first_ref, bf16[512,4096]{1,0:T(8,128)(2,1)} %q_ref.1, bf16[1024,512]{1,0:T(8,128)(2,1)} %k_ref.2, bf16[1024,512]{1,0:T(8,128)(2,1)} %v_ref.2, bf16[32,512]{1,0:T(8,128)(2,1)} %sk_ref.1, bf16[32,512]{1,0:T(8,128)(2,1)} %sv_ref.1), custom_call_target="tpu_custom_call" | custom-call | flops 8589934592 | bytes 10485760 | tf_op jit(solution)/shard_map/pallas_call | solution.py:75
  79.0 97.4 %shard_map.167 = bf16[8,40,4096]{2,1,0:T(8,128)(2,1)} custom-call(bf16[2,8,32,4096]{3,2,1,0:T(8,128)(2,1)} %bitcast.53, f32[2,8,32,128]{3,2,1,0:T(8,128)} %bitcast.63, bf16[8,8,4096]{2,1,0:T(8,128)(2,1)} %reshape.84.od_ref, f32[8,8,128]{2,1,0:T(8,128)} %pad_bitcast_fusion.ld_ref), custom_call_target="tpu_custom_call" | custom-call | tf_op jit(solution)/shard_map/pallas_call | solution.py:417
  176.4 0.0 copy-start
  176.5 8.2 %convolution_bitcast_fusion.p_ref = f32[2,320,512]{2,1,0:T(8,128)} fusion(bf16[320,4096,1]{1,0,2:T(8,128)(2,1)} %bitcast.54, bf16[2,512,4096]{2,1,0:T(8,128)(2,1)} %bitcast.52), kind=kOutput, calls=%fused_computation.1 | convolution fusion | flops 2684354560 | bytes 12320768 | tf_op jit(solution)/shard_map/dot_general | solution.py:508
  184.7 10.8 %shard_map.168 = bf16[320,512]{1,0:T(8,128)(2,1)} custom-call(f32[2,320,512]{2,1,0:T(8,128)} %convolution_bitcast_fusion.p_ref), custom_call_target="tpu_custom_call" | custom-call | tf_op jit(solution)/shard_map/pallas_call | solution.py:396
  195.4 1.7 slice.20
  197.1 1.5 slice.21
  198.6 0.0 copy-done
  198.6 0.2 convert_reduce_fusion
  198.8 0.0 all-gather.2.cloned.1.call-done
  198.8 1.7 reshape.91
  200.5 0.2 convolution_convert_fusion
  200.8 0.1 reshape.92
  200.9 0.2 fusion.5
  201.1 0.7 copy_bitcast_fusion.2
  (2 shorter events, 0.0 us)
Async XLA Ops:
  7.2 191.6 %all-gather.2.cloned.1.call-start = ((), (), s32[]{:S(2)}) async-start(), calls=%async_computation | async-start | bytes 1114112 | tf_op jit(solution)/shard_map/all_gather | solution.py:469
  176.4 22.1 %copy-start = (s32[128,1]{0,1:T(1,128)S(1)}, s32[128,1]{0,1:T(1,128)}, u32[]{:S(2)}) copy-start(s32[128,1]{0,1:T(1,128)} %param.27) | copy-start | bytes 1540
Sparse Core Ops, SparseCore 0:
  10.2 37.8 all-gather.1

commit v3 on v2

--- a/solution.py
+++ b/solution.py
@@ -507,6 +507,7 @@
     attention = attention.reshape(seq_count * (span_block + decode_block), width)
     partial = jnp.dot(attention, out_weight, preferred_element_type=jnp.float32)
     tensor_count = lax.axis_size("tensor")
+    partial = lax.optimization_barrier(partial)
     partial = partial.reshape(partial.shape[0], tensor_count, -1).transpose(1, 0, 2)
     part = add_tensor(tensor_count, partial).reshape(seq_count, span_block + decode_block, -1)
     prefill_out = part[:, :span_block].reshape(seq_count * span_block, -1)

time: 210 us -> 197 us (0.938)
  local copies, waits for them, and re-layouts: 26.7 us -> 16.6 us
  matrix products: 8.47 us -> 6.34 us
    dot_general x1 -> x0, local copies, waits for them, and re-layouts: 11.2 us -> none  [body(): partial = jnp.dot(attention, out_weight, preferred_element_type=jnp.float32)]
    dot_general x1, matrix products: 8.23 us -> 6.09 us  [body(): partial = jnp.dot(attention, out_weight, preferred_element_type=jnp.float32)]
  transfers between devices with their start and end apart: 1 -> 1, of which waited for: 0 -> 0; matrix products, arithmetic and copies ran while one was open for 16% -> 11% of each run, Pallas kernels for 75% -> 80%
where the time goes in v3:
time: 197 us
  Pallas kernels  156 us (79%)
  local copies, waits for them, and re-layouts  16.6 us (8%)
  between operations  14.1 us (7%)
  matrix products  6.34 us (3%)
  other arithmetic  2.94 us (1%)
    pallas_call x1, Pallas kernels, merge(): pl.pallas_call(functools.partial(merge_kernel, n, width // HEAD), out_sha...  97.5 us
    pallas_call x1, Pallas kernels, prefill_local(): pl.pallas_call(functools.partial(prefill_kernel, group_size, chunk), grid...  34.1 us
    pallas_call x1, Pallas kernels, decode_local(): pl.pallas_call(functools.partial(decode_kernel, HEADS // KV_HEADS), grid=...  14 us
    pallas_call x1, Pallas kernels, add_tensor(): pl.pallas_call(functools.partial(add_kernel, n), out_shape=jax.ShapeDtype...  10.8 us
    dot_general x1, matrix products, body(): partial = jnp.dot(attention, out_weight, preferred_element_type=jnp.float32)  6.09 us
  transfers between devices with their start and end apart: 1, of which 0 were waited for; matrix products, arithmetic and copies ran while one was open for 11% of the time, Pallas kernels for 80%

profile of v3, /device:TPU:26, one launch (start us, length us, event | category | flops | bytes accessed | tf_op | source)
XLA Modules:
  0.0 196.5 jit_solution(11571347291968325328)
XLA Ops:
  7.2 0.0 all-gather.2.cloned.1.call-start
  7.2 1.4 pad_maximum_fusion
  8.6 0.0 all-gather.2.cloned.1.call-update
  8.6 0.9 reshape.82
  9.5 0.9 reshape.83
  10.4 1.1 copy.47
  11.5 0.9 copy.56
  12.5 0.8 copy_bitcast_fusion.4
  13.2 1.4 select_reduce_fusion.length_ref
  14.6 14.0 %shard_map.166 = (bf16[16,4,32,128]{3,2,1,0:T(8,128)(2,1)}, f32[16,4,32,128]{3,2,1,0:T(8,128)}) custom-call(s32[16]{0:T(128)} %select_reduce_fusion.length_ref, s32[1]{0:T(128)} %bitcast.3.where_ref, bf16[16,4,32,128]{3,2,1,0:T(8,128)(2,1)} %bitcast.55, bf16[16,256,512]{2,1,0:T(8,128)(2,1)} %k_ref.3, bf16[16,256,512]{2,1,0:T(8,128)(2,1)} %v_ref.3, ...), custom_call_target="tpu_custom_call" | custom-call | flops 268435456 | bytes 8388608 | tf_op jit(solution)/shard_map/pallas_call | solution.py:148
  28.6 1.1 copy_bitcast_fusion
  29.7 1.1 reshape.85.od_ref
  30.8 2.1 %copy.37 = f32[16,4,32,1]{0,2,1,3:T(8,128)S(1)} copy(f32[16,4,32,1]{3,2,1,0:T(8,128)} %bitcast.60) | data formatting | bytes 16384 | tf_op jit(solution)/shard_map/slice | solution.py:501
  32.9 0.1 reshape.86
  33.0 0.1 copy.45
  33.0 0.6 pad_bitcast_fusion.ld_ref
  33.7 34.1 %shard_map.165 = (bf16[512,4096]{1,0:T(8,128)(2,1)}, f32[512,128]{1,0:T(8,128)}) custom-call(s32[1]{0:T(128)} %bitcast.first_ref, bf16[512,4096]{1,0:T(8,128)(2,1)} %q_ref.1, bf16[1024,512]{1,0:T(8,128)(2,1)} %k_ref.2, bf16[1024,512]{1,0:T(8,128)(2,1)} %v_ref.2, bf16[32,512]{1,0:T(8,128)(2,1)} %sk_ref.1, bf16[32,512]{1,0:T(8,128)(2,1)} %sv_ref.1), custom_call_target="tpu_custom_call" | custom-call | flops 8589934592 | bytes 10485760 | tf_op jit(solution)/shard_map/pallas_call | solution.py:75
  67.8 97.5 %shard_map.167 = bf16[8,40,4096]{2,1,0:T(8,128)(2,1)} custom-call(bf16[2,8,32,4096]{3,2,1,0:T(8,128)(2,1)} %bitcast.53, f32[2,8,32,128]{3,2,1,0:T(8,128)} %bitcast.64, bf16[8,8,4096]{2,1,0:T(8,128)(2,1)} %reshape.85.od_ref, f32[8,8,128]{2,1,0:T(8,128)} %pad_bitcast_fusion.ld_ref), custom_call_target="tpu_custom_call" | custom-call | tf_op jit(solution)/shard_map/pallas_call | solution.py:417
  165.3 6.1 %fusion.6 = f32[320,1024]{1,0:T(8,128)S(1)} fusion(bf16[320,4096]{1,0:T(8,128)(2,1)} %bitcast.54, bf16[4096,1024]{1,0:T(8,128)(2,1)} %param.19), kind=kOutput, calls=%fused_computation.21 | convolution fusion | flops 2684354560 | bytes 12320768 | tf_op jit(solution)/shard_map/dot_general | solution.py:508
  171.4 0.0 copy-start
  171.4 1.2 copy.55
  172.6 10.8 %shard_map.168 = bf16[320,512]{1,0:T(8,128)(2,1)} custom-call(f32[2,320,512]{2,1,0:T(8,128)} %bitcast.52), custom_call_target="tpu_custom_call" | custom-call | tf_op jit(solution)/shard_map/pallas_call | solution.py:396
  183.3 1.7 slice.20
  185.0 1.5 slice.21
  186.5 0.0 copy-done
  186.5 0.2 convert_reduce_fusion
  186.7 0.0 all-gather.2.cloned.1.call-done
  186.7 1.7 reshape.93
  188.4 0.2 convolution_convert_fusion
  188.7 0.1 reshape.94
  188.8 0.2 fusion.5
  189.0 0.7 copy_bitcast_fusion.2
  (2 shorter events, 0.0 us)
Async XLA Ops:
  7.2 179.5 %all-gather.2.cloned.1.call-start = ((), (), s32[]{:S(2)}) async-start(), calls=%async_computation | async-start | bytes 1114112 | tf_op jit(solution)/shard_map/all_gather | solution.py:469
  171.4 15.1 %copy-start = (s32[128,1]{0,1:T(1,128)S(1)}, s32[128,1]{0,1:T(1,128)}, u32[]{:S(2)}) copy-start(s32[128,1]{0,1:T(1,128)} %param.27) | copy-start | bytes 1540
Sparse Core Ops, SparseCore 0:
  10.2 37.8 all-gather.1
